TPU v7x, 128 devices: a whole 4x4x4 slice. The times are simulated.
128 devices in a mesh: tm: 16 (over y, x), lane: 8 (over z, core).
Axes of the slice: x: 4, y: 4, z: 4, core: 2. Of those that a mesh axis runs over, the one named last changes fastest.
Arguments:
- replay: bfloat16 [8, 16, 1024, 1024], P('lane', 'tm'), may hold values from -6 to 6
- block_owner: int32 [16, 8, 8, 1], P('tm'), may hold values from 0 to 7; in each aligned block of 8 rows (0 to 7, 8 to 15, ..., all dimensions but the last counted through in order) at most 2 rows name the same one
- block_slot: int32 [16, 8, 8], P('tm'), may hold values from 0 to 3
- block_fill: int32 [8, 16, 8], P('lane', 'tm'), may hold values from 64 to 256
- log_decay: float32 [8, 16, 32768], P('lane', None, 'tm'), may hold values from -2 to 0
- resets: int32 [8, 32768], P('lane', 'tm'), may hold values from 0 to 1, as said below
- cotangent: bfloat16 [8, 32768, 1024], P('lane', 'tm'), may hold values from -6 to 6
- w_in: bfloat16 [1024, 1024], replicated, may hold values from -0.1875 to 0.1875
- w_bc: bfloat16 [1024, 128], replicated, may hold values from -0.01171875 to 0.01171875
- w_out: bfloat16 [1024, 1024], replicated, may hold values from -0.1875 to 0.1875
Outputs:
- grad_in: float32 [1024, 1024], P(('tm', 'lane'))
- grad_bc: float32 [1024, 128], P(('tm', 'lane'))
- grad_out: float32 [1024, 1024], P(('tm', 'lane'))
Inputs may be any that keep to these rules, and one draw needn't show every extreme that they name: `block_owner`: among the 8 blocks of one segment on one time shard, no owner is named more than 2 times. `resets`: exactly one step of each segment is flagged.
All inputs are finite; a program needn't handle non-finite values.
Results may differ from a plain program's by a relative error of at most 0.0057.
Values may be sent and summed in bfloat16 or wider, within the bound.
No kernel may reach another device: no remote copies, remote signals or barrier semaphores. Data moves between devices by JAX's collectives and lax.ppermute only.
A program may use at most 192 MiB of HBM per device.

v0:
```python
import math

import jax
import jax.numpy as jnp
from jax import lax
from jax.sharding import Mesh
from jax.sharding import PartitionSpec as P

D = 1024
HEAD = 64
STATE = 64
BLOCK = 256
BUFCH = 4
TOK_DEV = 2048
TM = ("tm_0", "tm_1")
TM_LANE = ("tm_0", "tm_1", "lane")


def neutral_like(x, identity):
    return jax.tree.map(
        lambda part, zero: jnp.zeros_like(part) + jnp.asarray(zero, part.dtype), x, identity
    )


def carried_in_2(x, axes, combine, identity, reverse):
    before = start = neutral_like(x, identity)
    subtotal = x
    for axis in reversed(axes):
        peers, mine = (lax.axis_size(axis), lax.axis_index(axis))
        pieces = jax.tree.map(lambda part: lax.all_gather(part, axis), subtotal)
        inside, subtotal = (start, start)
        for k in reversed(range(peers)) if reverse else range(peers):
            passed = k > mine if reverse else k < mine
            subtotal = combine(subtotal, jax.tree.map(lambda part: part[k], pieces))
            inside = jax.tree.map(lambda new, old: jnp.where(passed, new, old), subtotal, inside)
        before = combine(inside, before)
    return before


def decay_matrix(log_rate, episode_flags):
    cumulated = jnp.cumsum(log_rate, axis=1)
    counted = jnp.cumsum(episode_flags)
    extent = log_rate.shape[1]
    row_pos = lax.broadcasted_iota(jnp.int32, (extent, extent), 0)
    col_pos = lax.broadcasted_iota(jnp.int32, (extent, extent), 1)
    linked = (counted[:, None] == counted[None, :]) & (col_pos <= row_pos)
    spread = jnp.where(linked[None], cumulated[:, :, None] - cumulated[:, None, :], 0.0)
    return jnp.where(linked[None], jnp.exp(spread), 0.0)


def edge_weights(log_rate, episode_flags):
    cumulated = jnp.cumsum(log_rate, axis=1)
    counted = jnp.cumsum(episode_flags)
    opening = jnp.where(counted[None, :] == 0, jnp.exp(cumulated), 0.0)
    closing = jnp.where(
        counted[None, :] == counted[-1], jnp.exp(cumulated[:, -1:] - cumulated), 0.0
    )
    return (opening, closing)


def product(spec, left_op, right_op):
    return jnp.einsum(spec, left_op, right_op, preferred_element_type=jnp.float32)


def block_grads(block_items):
    (
        inner_proj,
        write_keys,
        read_keys,
        upstream,
        log_rate,
        episode_flags,
        opening,
        closing,
        weighted_in,
        weighted_out,
        start_state,
        end_adjoint,
    ) = block_items
    extent = inner_proj.shape[0]
    decays = decay_matrix(log_rate, episode_flags)
    scores = lax.dot_general(
        read_keys, write_keys, (((1,), (1,)), ((), ())), preferred_element_type=jnp.float32
    )
    mixing = (decays * scores[None]).astype(jnp.bfloat16)
    state_bf = start_state.astype(jnp.bfloat16)
    adjoint_bf = end_adjoint.astype(jnp.bfloat16)
    carried = product("in,hpn->ihp", read_keys, state_bf)
    readout = product("hij,jhp->ihp", mixing, inner_proj) + opening.T[:, :, None] * carried
    pairing = product("ihp,jhp->hij", upstream, inner_proj)
    blended = (decays * pairing).astype(jnp.bfloat16)
    returned = product("jn,hpn->jhp", write_keys, adjoint_bf)
    grad_inner = product("hij,ihp->jhp", mixing, upstream) + closing.T[:, :, None] * returned
    grad_write = product("hij,in->jn", blended, read_keys) + product(
        "jhp,hpn->jn", weighted_in, adjoint_bf
    )
    grad_read = product("hij,jn->in", blended, write_keys) + product(
        "ihp,hpn->in", weighted_out, state_bf
    )
    return (
        readout.astype(jnp.bfloat16).reshape(extent, -1),
        grad_inner.astype(jnp.bfloat16).reshape(extent, -1),
        jnp.concatenate([grad_write, grad_read], axis=1).astype(jnp.bfloat16),
    )


def advance(carried_in, block_items):
    current, gained = carried_in
    block_factor, pushed = block_items
    return (
        (block_factor[:, None, None] * current + pushed, gained * block_factor),
        (current, gained),
    )


def combine(former, latter):
    return (former[0] * latter[0], latter[0][:, None, None] * former[1] + latter[1])


def on_device(
    replay, block_owner, block_slot, block_fill, log_decay, resets, cotangent, w_in, w_bc, w_out
):
    lane_count = lax.axis_size("lane")
    shards = lax.axis_size(TM)
    my_lane = lax.axis_index("lane")
    num_heads = D // HEAD
    blocks = block_fill.shape[2]
    owners = block_owner[0, :, :, 0]
    slot_map = block_slot[0]
    my_owner = lax.dynamic_index_in_dim(owners, my_lane, 0, keepdims=False)
    my_slot = lax.dynamic_index_in_dim(slot_map, my_lane, 0, keepdims=False)
    portion = lax.all_gather(replay, "lane", axis=0, tiled=True)
    amount = portion.shape[0]
    flat = portion.reshape(amount * BUFCH, BLOCK * D)
    position = my_owner * BUFCH + my_slot
    choose = (
        lax.broadcasted_iota(jnp.int32, (blocks, amount * BUFCH), 1) == position[:, None]
    ).astype(jnp.bfloat16)
    delivered = jnp.dot(choose, flat, preferred_element_type=jnp.float32).astype(jnp.bfloat16)
    usable = (
        lax.broadcasted_iota(jnp.int32, (blocks, BLOCK), 1) < block_fill[0, 0][:, None]
    ).reshape(blocks * BLOCK)
    delivered = jnp.where(
        usable[:, None], delivered.reshape(blocks * BLOCK, D), jnp.zeros((), jnp.bfloat16)
    )
    masked = jnp.where(usable[:, None], cotangent[0], jnp.zeros((), jnp.bfloat16))
    inner_proj = jnp.dot(delivered, w_in, preferred_element_type=jnp.float32).astype(jnp.bfloat16)
    projected = jnp.dot(delivered, w_bc, preferred_element_type=jnp.float32).astype(jnp.bfloat16)
    upstream = lax.dot_general(
        masked, w_out, (((1,), (1,)), ((), ())), preferred_element_type=jnp.float32
    ).astype(jnp.bfloat16)
    inner_b = inner_proj.reshape(blocks, BLOCK, num_heads, HEAD)
    upstream_b = upstream.reshape(blocks, BLOCK, num_heads, HEAD)
    write_b = projected[:, :STATE].reshape(blocks, BLOCK, STATE)
    read_b = projected[:, STATE:].reshape(blocks, BLOCK, STATE)
    rates_b = jnp.transpose(log_decay[0].reshape(num_heads, blocks, BLOCK), (1, 0, 2))
    flags_b = resets[0].reshape(blocks, BLOCK)
    opening, closing = jax.vmap(edge_weights)(rates_b, flags_b)
    factor = opening[:, :, -1]
    weighted_in = (jnp.transpose(closing, (0, 2, 1))[..., None] * inner_b).astype(jnp.bfloat16)
    weighted_out = (jnp.transpose(opening, (0, 2, 1))[..., None] * upstream_b).astype(jnp.bfloat16)
    push_fwd = product("kjhp,kjn->khpn", weighted_in, write_b)
    push_bwd = product("kihp,kin->khpn", weighted_out, read_b)
    zero_state = jnp.zeros((num_heads, HEAD, STATE), jnp.float32)
    unit_gain = jnp.ones((num_heads,), jnp.float32)
    (dev_state, dev_gain), (local_start, prefix_gain) = lax.scan(
        advance, (zero_state, unit_gain), (factor, push_fwd)
    )
    (dev_back, dev_gain_back), (local_end, suffix_gain) = lax.scan(
        advance, (zero_state, unit_gain), (factor, push_bwd), reverse=True
    )
    enter_state = carried_in_2((dev_gain, dev_state), TM, combine, (unit_gain, zero_state), False)[
        1
    ]
    enter_adjoint = carried_in_2(
        (dev_gain_back, dev_back), TM, combine, (unit_gain, zero_state), True
    )[1]
    starts = local_start + prefix_gain[:, :, None, None] * enter_state
    ends = local_end + suffix_gain[:, :, None, None] * enter_adjoint
    readout, grad_inner, grad_keys = lax.map(
        block_grads,
        (
            inner_b,
            write_b,
            read_b,
            upstream_b,
            rates_b,
            flags_b,
            opening,
            closing,
            weighted_in,
            weighted_out,
            starts,
            ends,
        ),
    )
    readout = readout.reshape(blocks * BLOCK, D)
    grad_inner = grad_inner.reshape(blocks * BLOCK, D)
    grad_keys = grad_keys.reshape(blocks * BLOCK, 2 * STATE)
    grad_scale = 1.0 / math.sqrt(TOK_DEV * shards * lane_count)
    contract = (((0,), (0,)), ((), ()))
    summed = lax.psum_scatter(
        jnp.concatenate(
            [
                lax.dot_general(
                    delivered, grad_inner, contract, preferred_element_type=jnp.float32
                ),
                lax.dot_general(delivered, grad_keys, contract, preferred_element_type=jnp.float32),
                lax.dot_general(readout, masked, contract, preferred_element_type=jnp.float32),
            ],
            axis=1,
        )
        * grad_scale,
        TM_LANE,
        scatter_dimension=0,
        tiled=True,
    )
    return (summed[:, :D], summed[:, D : D + 2 * STATE], summed[:, D + 2 * STATE :])


def solution(mesh):
    torus = Mesh(mesh.devices.reshape(4, 4, mesh.shape["lane"]), ("tm_0", "tm_1", "lane"))
    return jax.shard_map(
        on_device,
        mesh=torus,
        in_specs=(
            P("lane", TM, None, None),
            P(TM, None, None, None),
            P(TM, None, None),
            P("lane", TM, None),
            P("lane", None, TM),
            P("lane", TM),
            P("lane", TM, None),
            P(),
            P(),
            P(),
        ),
        out_specs=(P(TM_LANE, None), P(TM_LANE, None), P(TM_LANE, None)),
        check_vma=False,
    )
```

profile of v0, /device:TPU:0, one launch (start us, length us, event | category | flops | bytes accessed | tf_op | source)
XLA Modules:
  0.0 661.0 jit_solution(18061745973087660398)
XLA Ops:
  13.2 4.6 reduce-window.31
  19.7 9.2 %fusion.72 = bf16[2048,1024]{1,0:T(8,128)(2,1)} fusion(bf16[1024,1024]{1,0:T(8,128)(2,1)S(1)} %copy-done, bf16[1,2048,1024]{2,1,0:T(8,128)(2,1)} %param.22, pred[2048]{0:T(1024)(128)(4,1)} %lt.64), kind=kOutput, calls=%fused_computation.108 | convolution fusion | flops 4299161600 | bytes 10487808 | tf_op jit(solution)/shard_map/dot_general | solution.py:149
  28.9 6.5 copy.108
  35.4 5.8 copy.149
  42.1 5.0 multiply_convert_fusion.8
  47.1 50.3 %all-gather.12.cloned.1.call-done = bf16[8,1,1024,1024]{3,2,1,0:T(8,128)(2,1)} async-done(((bf16[1,1,1024,1024]{3,2,1,0:T(8,128)(2,1)}), bf16[8,1,1024,1024]{3,2,1,0:T(8,128)(2,1)}) %all-gather.12.cloned.1.call-update) | async-done | bytes 16777232 | tf_op jit(solution)/shard_map/all_gather | solution.py:132
  97.4 15.0 %reshape.369 = bf16[32,262144]{1,0:T(8,128)(2,1)} reshape(bf16[8,1,1024,1024]{3,2,1,0:T(8,128)(2,1)} %all-gather.12.cloned.1.call-done) | data formatting | bytes 33554432 | tf_op jit(solution)/shard_map/reshape | solution.py:134
  113.3 11.4 %broadcast_select_fusion.3 = (bf16[8,262144]{1,0:T(8,128)(2,1)}, bf16[8,262144]{1,0:T(8,128)(2,1)}) fusion(pred[8,262144]{1,0:T(8,128)(4,1)S(1)} %bitcast.373, bf16[32,262144]{1,0:T(8,128)(2,1)} %reshape.369, s32[8]{0:T(128)S(1)} %bitcast_add_fusion.2), kind=kOutput, calls=%fused_computation.113 | convolution fusion | flops 138412288 | bytes 27263008 | tf_op jit(solution)/shard_map/dot_general | solution.py:139
  124.8 6.2 reshape.370
  131.0 8.6 %convolution_convert_fusion.1 = bf16[2048,1024]{1,0:T(8,128)(2,1)} fusion(bf16[1024,1024]{1,0:T(8,128)(2,1)S(1)} %copy-done.25, bf16[2048,1024]{1,0:T(8,128)(2,1)} %reshape.370, pred[2048]{0:T(1024)(128)(4,1)S(1)} %copy-done.21), kind=kOutput, calls=%fused_computation.109 | convolution fusion | flops 4299161600 | bytes 10487808 | tf_op jit(solution)/shard_map/dot_general | solution.py:147
  139.6 6.6 copy.99
  146.2 5.8 copy.146
  154.2 3.3 fusion.91
  157.5 2.5 broadcast.199.clone.1
  160.0 16.7 %while.54 = (s32[]{:T(128)}, f32[16,64,64]{2,1,0:T(8,128)S(1)}, f32[16]{0:T(128)S(1)}, f32[8,16,64,64]{3,2,1,0:T(8,128)}, f32[8,16]{1,0:T(8,128)S(1)}, /*index=5...) while((s32[]{:T(128)}, f32[16,64,64]{2,1,0:T(8,128)S(1)}, ...), condition=%wide.region_7.8_spmd.clone, body=%wide.region_6.7_spmd.clone.sunk | while | flops 262180 | bytes 1573517 | solution.py:169
  177.8 3.1 multiply_convert_fusion.9
  180.9 3.3 fusion.93
  184.2 2.5 broadcast.199.clone
  186.7 16.6 %while.53 = (s32[]{:T(128)}, f32[16,64,64]{2,1,0:T(8,128)S(1)}, f32[16]{0:T(128)S(1)}, f32[8,16,64,64]{3,2,1,0:T(8,128)}, f32[8,16]{1,0:T(8,128)S(1)}, /*index=5...) while((s32[]{:T(128)}, f32[16,64,64]{2,1,0:T(8,128)S(1)}, ...), condition=%wide.region_5.6_spmd.clone, body=%wide.region_4.5_spmd.clone.sunk | while | flops 262179 | bytes 1574005 | solution.py:166
  206.0 10.4 %all-reduce.3 = (f32[64]{0:T(128)S(1)}, f32[64]{0:T(128)S(1)}) all-reduce(f32[64]{0:T(128)S(1)} %dynamic-update-slice, f32[64]{0:T(128)S(1)} %dynamic-update-slice.1), channel_id=2, replica_groups=mesh['tm_0'=4,'tm_1'=4,'lane'=8] {'tm_1'}, use_global_device_ids=true, to_apply=%add | all-reduce | flops 128 | bytes 1024
  216.5 2.5 fusion.79
  219.2 22.3 %all-gather.18.cloned.1.call-done = f32[64,64,64]{2,1,0:T(8,128)} async-done(((f32[16,64,64]{2,1,0:T(8,128)}), f32[64,64,64]{2,1,0:T(8,128)}) %all-gather.18.cloned.1.call-update) | async-done | bytes 1048592 | tf_op jit(solution)/shard_map/all_gather | solution.py:30
  241.5 2.5 fusion.87
  244.1 5.4 copy.110
  249.5 2.9 copy.116
  253.6 5.4 copy.106
  259.0 3.0 copy.112
  262.0 6.3 select_n.235
  268.3 9.7 %all-gather.5 = f32[4,1,16]{2,1,0:T(1,128)S(1)} all-gather(f32[1,1,16]{2,1,0:T(1,128)S(1)} %get-tuple-element.494), channel_id=1, replica_groups=mesh['tm_0'=4,'tm_1'=4,'lane'=8] {'tm_0'}, dimensions={0}, use_global_device_ids=true | all-gather | bytes 320 | tf_op jit(solution)/shard_map/all_gather | solution.py:30
  277.9 7.3 %all-gather.4 = f32[4,1,16]{2,1,0:T(1,128)S(1)} all-gather(f32[1,1,16]{2,1,0:T(1,128)S(1)} %get-tuple-element.500), channel_id=1, replica_groups=mesh['tm_0'=4,'tm_1'=4,'lane'=8] {'tm_0'}, dimensions={0}, use_global_device_ids=true | all-gather | bytes 320 | tf_op jit(solution)/shard_map/all_gather | solution.py:30
  285.4 2.7 fusion.78
  288.3 1.8 multiply_add_fusion
  290.2 16.1 %all-gather.14.cloned.1.call-done = f32[4,16,64,64]{3,2,1,0:T(8,128)} async-done(((f32[1,16,64,64]{3,2,1,0:T(8,128)}), f32[4,16,64,64]{3,2,1,0:T(8,128)}) %all-gather.14.cloned.1.call-update) | async-done | bytes 1048592 | tf_op jit(solution)/shard_map/all_gather | solution.py:30
  306.3 2.6 fusion.86
  309.1 1.9 multiply_add_fusion.1
  311.0 155.7 %while.52 = (s32[]{:T(128)}, bf16[8,256,1024]{2,1,0:T(8,128)(2,1)}, bf16[8,256,1024]{2,1,0:T(8,128)(2,1)}, bf16[8,256,128]{2,1,0:T(8,128)(2,1)}, bf16[8,256,16,6...) while((s32[]{:T(128)}, bf16[8,256,1024]{2,1,0:T(8,128)(2,1)}, ...), condition=%wide.region_14.15_spmd, body=%wide.region_8.14_spmd.sunk | while | flops 582320192 | bytes 16335565 | solution.py:180
  313.8 2.4 fusion.175
  319.2 2.4 fusion.173
  323.9 2.7 convert_reduce_fusion.2
  333.2 2.4 fusion.175
  338.7 2.4 fusion.173
  343.4 2.7 convert_reduce_fusion.2
  352.7 2.4 fusion.175
  358.1 2.4 fusion.173
  362.9 2.7 convert_reduce_fusion.2
  372.1 2.4 fusion.175
  377.6 2.4 fusion.173
  382.3 2.7 convert_reduce_fusion.2
  391.6 2.4 fusion.175
  397.0 2.4 fusion.173
  401.8 2.7 convert_reduce_fusion.2
  411.0 2.4 fusion.175
  416.5 2.4 fusion.173
  421.2 2.7 convert_reduce_fusion.2
  430.5 2.4 fusion.175
  436.0 2.4 fusion.173
  440.7 2.7 convert_reduce_fusion.2
  450.0 2.4 fusion.175
  455.4 2.4 fusion.173
  460.2 2.7 convert_reduce_fusion.2
  466.8 7.9 %fusion.110 = f32[1024,1024]{0,1:T(8,128)S(1)} fusion(bf16[2048,1024]{1,0:T(8,128)(2,1)} %select_n.235, bf16[2048,1024]{1,0:T(8,128)(2,1)} %bitcast.390), kind=kOutput, calls=%fused_computation.202 | convolution fusion | flops 4294967296 | bytes 12582912 | tf_op jit(solution)/shard_map/dot_general | solution.py:205
  476.9 4.9 fusion.66
  481.8 4.0 maximum_multiply_fusion
  485.9 163.4 %all-reduce.6.cloned.1.call-done = f32[1024,2176]{0,1:T(8,128)} async-done(((f32[1024,2176]{0,1:T(8,128)}), f32[1024,2176]{0,1:T(8,128)}) %all-reduce.6.cloned.1.call-update) | async-done | bytes 8912912
  (426 shorter events, 151.4 us)
Async XLA Ops:
  7.2 12.5 %copy-start = (bf16[1024,1024]{1,0:T(8,128)(2,1)S(1)}, bf16[1024,1024]{1,0:T(8,128)(2,1)}, u32[]{:S(2)}) copy-start(bf16[1024,1024]{1,0:T(8,128)(2,1)} %param.25) | copy-start | bytes 6291460
  7.2 90.2 %all-gather.12.cloned.1.call-start = ((), (), s32[]{:S(2)}) async-start(), calls=%async_computation | async-start | bytes 18874368 | tf_op jit(solution)/shard_map/all_gather | solution.py:132
  7.9 208.6 %all-gather.20.cloned.1.call-start = ((), (), s32[]{:S(2)}) async-start(), calls=%async_computation.4 | async-start | bytes 2621440 | tf_op jit(solution)/shard_map/all_gather | solution.py:30
  12.5 0.6 copy-start.16
  18.9 10.0 %copy-start.17 = (f32[8,16,256]{2,1,0:T(8,128)}, f32[8,16,256]{2,1,0:T(8,128)S(1)}, u32[]{:S(2)}) copy-start(f32[8,16,256]{2,1,0:T(8,128)S(1)} %get-tuple-element.776) | copy-start | bytes 393220
  47.1 65.4 %copy-start.19 = (pred[8,256]{0,1:T(8,128)(4,1)S(1)}, pred[8,256]{0,1:T(8,128)(4,1)}, u32[]{:S(2)}) copy-start(pred[8,256]{0,1:T(8,128)(4,1)} %copy.98) | copy-start | bytes 6148
  124.8 6.2 copy-start.21
  124.8 6.2 copy-start.25
  146.2 5.8 copy-start.13
  146.2 5.8 copy-start.27
  152.0 2.2 copy-start.4
  153.9 3.6 copy-start.14
  160.0 17.8 %copy-start.18 = (f32[8,256,16]{1,0,2:T(8,128)S(1)}, f32[8,256,16]{1,0,2:T(8,128)}, u32[]{:S(2)}) copy-start(f32[8,256,16]{1,0,2:T(8,128)} %copy.105) | copy-start | bytes 393220
  176.7 0.8 copy-start.3
  177.5 64.0 %all-gather.18.cloned.1.call-start = ((), (), s32[]{:S(2)}) async-start(), calls=%async_computation.3 | async-start | bytes 2621440 | tf_op jit(solution)/shard_map/all_gather | solution.py:30
  180.9 3.3 copy-start.5
  186.7 17.6 %copy-start.28 = (u32[128]{0:T(128)S(1)}, u32[128]{0:T(128)}, u32[]{:S(2)}) copy-start(u32[128]{0:T(128)} %constant.144) | copy-start | bytes 1540
  203.4 0.8 copy-start.2
  204.2 81.1 %all-gather.16.cloned.1.call-start = ((), (), s32[]{:S(2)}) async-start(), calls=%async_computation.2 | async-start | bytes 2621440 | tf_op jit(solution)/shard_map/all_gather | solution.py:30
  219.0 87.3 %all-gather.14.cloned.1.call-start = ((), (), s32[]{:S(2)}) async-start(), calls=%async_computation.1 | async-start | bytes 2621440 | tf_op jit(solution)/shard_map/all_gather | solution.py:30
  244.0 405.2 %all-reduce.6.cloned.1.call-start = ((), (), s32[]{:S(2)}) async-start(), calls=%async_computation.5 | async-start | bytes 17825792
  244.1 5.4 copy-start.6
  249.5 3.5 copy-start.20
  253.6 5.4 copy-start.7
  262.0 23.2 %copy-start.15 = (bf16[2048,64]{0,1:T(8,128)(2,1)S(1)}, bf16[2048,64]{0,1:T(8,128)(2,1)}, u32[]{:S(2)}) copy-start(bf16[2048,64]{0,1:T(8,128)(2,1)} %copy-done.14) | copy-start | bytes 786436
  262.0 23.3 %copy-start.10 = (f32[64,64,64]{2,1,0:T(8,128)S(1)}, f32[64,64,64]{2,1,0:T(8,128)}, u32[]{:S(2)}) copy-start(f32[64,64,64]{2,1,0:T(8,128)} %all-gather.20.cloned.1.call-done) | copy-start | bytes 3145732
  285.3 3.0 copy-start.8
  288.1 18.2 %copy-start.11 = (f32[64,64,64]{2,1,0:T(8,128)S(1)}, f32[64,64,64]{2,1,0:T(8,128)}, u32[]{:S(2)}) copy-start(f32[64,64,64]{2,1,0:T(8,128)} %all-gather.18.cloned.1.call-done) | copy-start | bytes 3145732
  306.3 2.8 copy-start.9
  466.8 8.0 %copy-start.12 = (bf16[2048,1024]{1,0:T(8,128)(2,1)S(1)}, bf16[2048,1024]{1,0:T(8,128)(2,1)}, u32[]{:S(2)}) copy-start(bf16[2048,1024]{1,0:T(8,128)(2,1)} %select_n.235) | copy-start | bytes 12582916
  466.8 8.0 %copy-start.26 = (bf16[8,256,128]{2,1,0:T(8,128)(2,1)S(1)}, bf16[8,256,128]{2,1,0:T(8,128)(2,1)}, u32[]{:S(2)}) copy-start(bf16[8,256,128]{2,1,0:T(8,128)(2,1)} %get-tuple-element.280) | copy-start | bytes 1572868
  466.8 8.8 %copy-start.24 = (bf16[8,256,1024]{2,1,0:T(8,128)(2,1)S(1)}, bf16[8,256,1024]{2,1,0:T(8,128)(2,1)}, u32[]{:S(2)}) copy-start(bf16[8,256,1024]{2,1,0:T(8,128)(2,1)} %get-tuple-element.281) | copy-start | bytes 12582916
  474.7 0.9 copy-start.22
  474.7 2.2 copy-start.23
  485.8 168.1 %copy-start.1 = (bf16[1024,1024]{1,0:T(8,128)(2,1)S(1)}, bf16[1024,1024]{1,0:T(8,128)(2,1)}, u32[]{:S(2)}) copy-start(bf16[1024,1024]{1,0:T(8,128)(2,1)} %param.25) | copy-start | bytes 6291460
Sparse Core Ops, SparseCore 0:
  9.7 87.6 all-gather.11
  177.6 31.2 all-gather.19
  210.6 30.8 all-gather.17
  243.0 30.8 all-gather.15
  275.4 30.8 all-gather.13
  486.0 163.1 all-reduce.5
where the time goes:
time: 672 us; the launch traced here: 661 us
  waiting for transfers between devices  253 us (38%)
  matrix products  157 us (23%)
  local copies, waits for them, and re-layouts  130 us (19%)
  other arithmetic  76.4 us (11%)
  blocking collectives  27.4 us (4%)
  between operations  15.4 us (2%)
    unnamed x7, waiting for transfers between devices  164 us
    dot_general x74, matrix products, product(): jnp.einsum(spec, left_op, right_op, preferred_element_type=jnp.float32)  111 us
    all_gather x1, waiting for transfers between devices, on_device(): portion = lax.all_gather(replay, 'lane', axis=0, tiled=True)  50.3 us
    all_gather x4, waiting for transfers between devices, carried_in_2(): pieces = jax.tree.map(lambda part: lax.all_gather(part, axis), subtotal)  38.5 us
    dynamic_update_slice x48, local copies, waits for them, and re-layouts, on_device(): lax.map(block_grads, (inner_b, write_b, read_b, upstream_b, rates_b, flag...  22.9 us
    unnamed x72, local copies, waits for them, and re-layouts  20.8 us
    add x16, other arithmetic, advance(): block_factor[:, None, None] * current + pushed  18.6 us
    all_gather x2, blocking collectives, carried_in_2(): pieces = jax.tree.map(lambda part: lax.all_gather(part, axis), subtotal)  17 us
  transfers between devices with their start and end apart: 6, of which 4 were waited for; matrix products, arithmetic and copies ran while one was open for 15% of the time, Pallas kernels for 0%

commit v1 on v0

v1 whole, which is shorter than its diff:
```python
import math

import jax
import jax.numpy as jnp
from jax import lax
from jax.experimental import pallas as pl
from jax.experimental.pallas import tpu as pltpu
from jax.sharding import Mesh
from jax.sharding import PartitionSpec as P

D = 1024
HEAD = 64
HEADS = 16
STATE = 64
BLOCK = 256
BUFCH = 4
TM = ("y", "x")
LOG2E = math.log2(math.e)
FAR = -1e4
F32, BF16 = jnp.float32, jnp.bfloat16
CNT, OPEN, CLOSE = 16, 32, 48
NT = (((1,), (1,)), ((), ()))
TN = (((0,), (0,)), ((), ()))
NN = (((1,), (0,)), ((), ()))
VMEM_LIMIT = 56 * 1024 * 1024


def mm(a, b, dims=NN):
    return lax.dot_general(a, b, dims, preferred_element_type=F32)


def split(x):
    high = x.astype(BF16)
    return jnp.concatenate([high, (x - high.astype(F32)).astype(BF16)], axis=1)


def spread_matrix(base):
    row = lax.broadcasted_iota(jnp.int32, (2 * 128, D), 0) & 127
    head = lax.broadcasted_iota(jnp.int32, (2 * 128, D), 1) >> 6
    return jnp.where(row == head + base, 1.0, 0.0).astype(BF16)


def call(kernel, name, out_shape, grid_spec, flops, nbytes):
    return pl.pallas_call(
        kernel,
        out_shape=out_shape,
        grid_spec=grid_spec,
        name=name,
        compiler_params=pltpu.CompilerParams(vmem_limit_bytes=VMEM_LIMIT),
        cost_estimate=pl.CostEstimate(flops=flops, bytes_accessed=nbytes, transcendentals=0),
    )


def shape(dims, kind):
    return jax.ShapeDtypeStruct(dims, kind)


def valid_rows(fill, width):
    return lax.broadcasted_iota(jnp.int32, (BLOCK, width), 0) < fill


def upstream_kernel(fill, decay, resets, cot, w_out, up, rows, cols, gain):
    b = pl.program_id(0)
    upper = lax.broadcasted_iota(jnp.int32, (BLOCK, BLOCK), 0) <= lax.broadcasted_iota(
        jnp.int32, (BLOCK, BLOCK), 1
    )
    upper = jnp.where(upper, 1.0, 0.0)
    both = jnp.concatenate(
        [decay[...] * LOG2E, jnp.broadcast_to(resets[0].astype(F32), (8, BLOCK))], axis=0
    )
    summed = lax.dot_general(
        both, upper, NN, precision=lax.Precision.HIGHEST, preferred_element_type=F32
    )
    cum, count = summed[:HEADS], summed[HEADS : HEADS + 8]
    two = jnp.concatenate([count, count], axis=0)
    opening = jnp.where(two == 0.0, jnp.exp2(cum), 0.0)
    last = jnp.broadcast_to(cum[:, BLOCK - 1 :], (HEADS, BLOCK))
    last_two = jnp.broadcast_to(two[:, BLOCK - 1 :], (HEADS, BLOCK))
    closing = jnp.where(two == last_two, jnp.exp2(last - cum), 0.0)
    table = jnp.concatenate(
        [cum, two, opening, closing, jnp.zeros((64, BLOCK), F32)], axis=0
    )
    rows[...] = table[:32]
    turned = table.T
    cols[...] = turned
    end = jnp.broadcast_to(turned[BLOCK - 1 :], (8, 128))

    @pl.when(b == 0)
    def _():
        gain[...] = end

    @pl.when(b > 0)
    def _():
        gain[...] = gain[...] * end

    masked = jnp.where(valid_rows(fill[b], D), cot[0], jnp.zeros((), BF16))
    up[...] = mm(masked, w_out[...], NT).astype(BF16)


def project_kernel(
    place, fill, rows, w_in, w_bc, up, cols, inner, keys, starts, pushed, gains, total, spread_o, spread_c, state
):
    b = pl.program_id(0)

    @pl.when(b == 0)
    def _():
        spread_o[...] = spread_matrix(OPEN)
        spread_c[...] = spread_matrix(CLOSE)
        state[...] = jnp.zeros_like(state)

    taken = jnp.where(valid_rows(fill[b], D), rows[0], jnp.zeros((), BF16))
    x = mm(taken, w_in[...]).astype(BF16)
    k = mm(taken, w_bc[...]).astype(BF16)
    inner[...] = x
    keys[...] = k
    parts = split(cols[...])
    opening = mm(parts, spread_o[...])
    closing = mm(parts, spread_c[...])
    into = (closing * x.astype(F32)).astype(BF16)
    out = (opening * up[...].astype(F32)).astype(BF16)
    turned = k.astype(F32).T.astype(BF16)
    push_in = mm(turned[:STATE], into)
    push_out = mm(turned[STATE:], out)
    factor = opening[BLOCK - 1 :]
    before = jnp.where(b == 0, 1.0, state[128:129])
    starts[0] = state[:64]
    pushed[0] = push_out
    gains[0] = jnp.concatenate(
        [jnp.broadcast_to(factor, (8, D)), jnp.broadcast_to(before, (8, D))], axis=0
    )
    state[:64] = state[:64] * factor + push_in
    state[64:128] = state[64:128] + before * push_out
    state[128:] = jnp.broadcast_to(before * factor, (8, D))

    @pl.when(b == pl.num_programs(0) - 1)
    def _():
        total[...] = state[:128].astype(BF16)


def inside_kernel(inner, keys, up, rows, cols, ro, gi, pair):
    at = lax.broadcasted_iota(jnp.int32, (BLOCK, BLOCK), 0)
    to = lax.broadcasted_iota(jnp.int32, (BLOCK, BLOCK), 1)
    linked = (to <= at) & (cols[:, CNT : CNT + 1] == rows[CNT : CNT + 1, :])
    bias = jnp.where(linked, 0.0, FAR)
    k = keys[...]
    scores = mm(k[:, STATE:], k[:, :STATE], NT)
    left = lax.broadcasted_iota(jnp.int32, (BLOCK, 128), 1) < HEAD
    zero = jnp.zeros((), BF16)
    paired = jnp.zeros((BLOCK, BLOCK), F32)
    for q in range(HEADS // 2):
        lanes = slice(128 * q, 128 * q + 128)
        x, u = inner[:, lanes], up[:, lanes]
        readout = grad = None
        for s in range(2):
            h = 2 * q + s
            mine = left if s == 0 else ~left
            xs, us = jnp.where(mine, x, zero), jnp.where(mine, u, zero)
            decays = jnp.exp2(cols[:, h : h + 1] - rows[h : h + 1, :] + bias)
            mixing = (decays * scores).astype(BF16)
            paired = paired + decays * mm(us, x, NT)
            r, g = mm(mixing, xs), mm(mixing, us, TN)
            readout = r if s == 0 else readout + r
            grad = g if s == 0 else grad + g
        ro[:, lanes] = readout.astype(BF16)
        gi[:, lanes] = grad.astype(BF16)
    pair[0] = paired.astype(BF16)


def scan_kernel(which, terms, gain, entering, forth, wide):
    wide[...] = mm(split(gain[...]), spread_matrix(OPEN))
    shards = terms.shape[0]
    state = jnp.zeros((8, D), F32)
    for t in range(shards):
        forth[t] = state
        state = state * wide[t : t + 1] + terms[t].astype(F32)
    back = jnp.zeros((8, D), F32)
    ahead = jnp.full((8, D), which[0], jnp.int32) < shards // 2
    for t in reversed(range(shards)):
        entering[t] = jnp.where(ahead, forth[t], back).astype(BF16)
        back = back * wide[t : t + 1] + terms[t].astype(F32)


def gradient_kernel(
    place, fill, rows, cot, inner, up, keys, cols, ro, gi, pair, starts, pushed, gains, enter,
    grads, acc_in, acc_bc, acc_out, spread_o, spread_c, finish,
):
    step = pl.program_id(0)
    last = pl.num_programs(0) - 1
    b = last - step

    @pl.when(step == 0)
    def _():
        spread_o[...] = spread_matrix(OPEN)
        spread_c[...] = spread_matrix(CLOSE)
        finish[...] = enter[64:].astype(F32)
        acc_in[...] = jnp.zeros_like(acc_in)
        acc_bc[...] = jnp.zeros_like(acc_bc)
        acc_out[...] = jnp.zeros_like(acc_out)

    factor, before = gains[0, 0:1], gains[0, 8:9]
    start = (starts[0] + before * enter[:64].astype(F32)).astype(BF16)
    end = finish[...].astype(BF16)
    finish[...] = finish[...] * factor + pushed[0]
    parts = split(cols[...])
    opening = mm(parts, spread_o[...])
    closing = mm(parts, spread_c[...])
    k = keys[...]
    write, read = k[:, :STATE], k[:, STATE:]
    readout = (ro[...].astype(F32) + opening * mm(read, start)).astype(BF16)
    grad = (gi[...].astype(F32) + closing * mm(write, end)).astype(BF16)
    into = (closing * inner[...].astype(F32)).astype(BF16)
    out = (opening * up[...].astype(F32)).astype(BF16)
    g = pair[0]
    grad_write = mm(g, read, TN) + mm(into, end, NT)
    grad_read = mm(g, write) + mm(out, start, NT)
    grad_keys = jnp.concatenate([grad_write, grad_read], axis=1).astype(BF16)
    wide = valid_rows(fill[b], D)
    taken = jnp.where(wide, rows[0], jnp.zeros((), BF16))
    masked = jnp.where(wide, cot[0], jnp.zeros((), BF16))
    acc_in[...] += mm(taken, grad, TN)
    acc_bc[...] += mm(taken, grad_keys, TN)
    acc_out[...] += mm(readout, masked, TN)

    @pl.when(step == last)
    def _():
        scale = 1.0 / 512.0
        grads[:, :D] = (acc_in[...] * scale).astype(BF16)
        grads[:, D : D + 128] = (acc_bc[...] * scale).astype(BF16)
        grads[:, D + 128 :] = (acc_out[...] * scale).astype(BF16)


def on_device(
    replay, block_owner, block_slot, block_fill, log_decay, resets, cotangent, w_in, w_bc, w_out
):
    shards = lax.axis_size(TM)
    my_lane = lax.axis_index(("z", "c"))
    blocks = block_fill.shape[2]
    steps = blocks * BLOCK
    fill = block_fill[0, 0]
    owner = lax.dynamic_index_in_dim(block_owner[0, :, :, 0], my_lane, 0, keepdims=False)
    slot = lax.dynamic_index_in_dim(block_slot[0], my_lane, 0, keepdims=False)
    place = owner * BUFCH + slot

    gathered = lax.all_gather(replay[0, 0], ("z", "c"), axis=0, tiled=True)
    gathered = gathered.reshape(-1, BLOCK, D)

    whole = lambda *dims: pl.BlockSpec(dims, lambda b, *_: (0,) * len(dims))
    tall = lambda width: pl.BlockSpec((BLOCK, width), lambda b, *_: (b, 0))
    lead = lambda *dims: pl.BlockSpec((1, *dims), lambda b, *_: (b,) + (0,) * len(dims))
    table_rows = pl.BlockSpec((32, BLOCK), lambda b, *_: (0, b))

    up, rows, cols, gain = call(
        upstream_kernel,
        "upstream",
        (shape((steps, D), BF16), shape((32, steps), F32), shape((steps, 128), F32), shape((8, 128), F32)),
        pltpu.PrefetchScalarGridSpec(
            num_scalar_prefetch=1,
            grid=(blocks,),
            in_specs=[
                pl.BlockSpec((HEADS, BLOCK), lambda b, *_: (0, b)),
                pl.BlockSpec((1, 1, BLOCK), lambda b, *_: (b, 0, 0)),
                pl.BlockSpec((1, BLOCK, D), lambda b, *_: (0, b, 0)),
                whole(D, D),
            ],
            out_specs=[tall(D), table_rows, tall(128), whole(8, 128)],
        ),
        2 * steps * D * D,
        12 << 20,
    )(fill, log_decay[0], resets.reshape(blocks, 1, BLOCK), cotangent, w_out)
    all_gain = lax.all_gather(gain[:1], TM, axis=0, tiled=True)

    picked = pl.BlockSpec((1, BLOCK, D), lambda b, place, *_: (place[b], 0, 0))
    inner, keys, starts, pushed, gains, total = call(
        project_kernel,
        "project",
        (
            shape((steps, D), BF16),
            shape((steps, 128), BF16),
            shape((blocks, STATE, D), F32),
            shape((blocks, STATE, D), F32),
            shape((blocks, 16, D), F32),
            shape((128, D), BF16),
        ),
        pltpu.PrefetchScalarGridSpec(
            num_scalar_prefetch=2,
            grid=(blocks,),
            in_specs=[picked, whole(D, D), whole(D, 128), tall(D), tall(128)],
            out_specs=[tall(D), tall(128), lead(STATE, D), lead(STATE, D), lead(16, D), whole(128, D)],
            scratch_shapes=[
                pltpu.VMEM((256, D), BF16),
                pltpu.VMEM((256, D), BF16),
                pltpu.VMEM((136, D), F32),
            ],
        ),
        2 * steps * D * (D + 128 + 128 + 256),
        20 << 20,
    )(place, fill, gathered, w_in, w_bc, up, cols)

    ro, gi, pair = call(
        inside_kernel,
        "inside",
        (shape((steps, D), BF16), shape((steps, D), BF16), shape((blocks, BLOCK, BLOCK), BF16)),
        pl.GridSpec(
            grid=(blocks,),
            in_specs=[tall(D), tall(128), tall(D), table_rows, tall(128)],
            out_specs=[tall(D), tall(D), lead(BLOCK, BLOCK)],
        ),
        2 * blocks * HEADS * 3 * BLOCK**3,
        18 << 20,
    )(inner, keys, up, rows, cols)

    terms = lax.all_to_all(total.reshape(shards, 8, D), TM, 0, 0)
    entering = call(
        scan_kernel,
        "scan",
        shape((shards, 8, D), BF16),
        pltpu.PrefetchScalarGridSpec(
            num_scalar_prefetch=1,
            grid=(1,),
            in_specs=[whole(shards, 8, D), whole(shards, 128)],
            out_specs=whole(shards, 8, D),
            scratch_shapes=[pltpu.VMEM((shards, 8, D), F32), pltpu.VMEM((shards, D), F32)],
        ),
        1 << 20,
        1 << 20,
    )(lax.axis_index(TM).reshape(1), terms, all_gain)
    enter = lax.all_to_all(entering, TM, 0, 0).reshape(128, D)

    back = lambda spec: pl.BlockSpec(
        spec.block_shape, lambda s, *refs: spec.index_map(blocks - 1 - s, *refs)
    )
    grads = call(
        gradient_kernel,
        "gradient",
        shape((D, 2 * D + 128), BF16),
        pltpu.PrefetchScalarGridSpec(
            num_scalar_prefetch=2,
            grid=(blocks,),
            in_specs=[
                back(s)
                for s in (
                    picked,
                    pl.BlockSpec((1, BLOCK, D), lambda b, *_: (0, b, 0)),
                    tall(D),
                    tall(D),
                    tall(128),
                    tall(128),
                    tall(D),
                    tall(D),
                    lead(BLOCK, BLOCK),
                    lead(STATE, D),
                    lead(STATE, D),
                    lead(16, D),
                    whole(128, D),
                )
            ],
            out_specs=whole(D, 2 * D + 128),
            scratch_shapes=[
                pltpu.VMEM((D, D), F32),
                pltpu.VMEM((D, 128), F32),
                pltpu.VMEM((D, D), F32),
                pltpu.VMEM((256, D), BF16),
                pltpu.VMEM((256, D), BF16),
                pltpu.VMEM((STATE, D), F32),
            ],
        ),
        2 * steps * D * (2 * D + 128 + 512),
        40 << 20,
    )(place, fill, gathered, cotangent, inner, up, keys, cols, ro, gi, pair, starts, pushed, gains, enter)

    lanes = lax.axis_size(("z", "c"))
    part = grads.reshape(shards, lanes, 8, -1).transpose(1, 0, 2, 3)
    part = lax.all_to_all(part, ("z", "c"), 0, 0).astype(F32).sum(0)
    part = lax.all_to_all(part.astype(BF16), TM, 0, 0).astype(F32).sum(0)
    return (part[:, :D], part[:, D : D + 128], part[:, D + 128 :])


def solution(mesh):
    torus = Mesh(mesh.devices.reshape(4, 4, 4, 2), ("y", "x", "z", "c"))
    lane = ("z", "c")
    every = TM + lane
    return jax.shard_map(
        on_device,
        mesh=torus,
        in_specs=(
            P(lane, TM, None, None),
            P(TM, None, None, None),
            P(TM, None, None),
            P(lane, TM, None),
            P(lane, None, TM),
            P(lane, TM),
            P(lane, TM, None),
            P(),
            P(),
            P(),
        ),
        out_specs=(P(every, None), P(every, None), P(every, None)),
        check_vma=False,
    )
```

time: 672 us -> 292 us (0.43); the launches traced: 661 us -> 291 us
  waiting for transfers between devices: 253 us -> 75.2 us
  matrix products: 157 us -> 0 us
  local copies, waits for them, and re-layouts: 130 us -> 6.15 us
  Pallas kernels: 0 us -> 82.2 us
  other arithmetic: 76.4 us -> 4.37 us
  blocking collectives: 27.4 us -> 97.6 us
  starting transfers between devices: 0.45 us -> 11.8 us
    unnamed x7 -> x1, waiting for transfers between devices: 164 us -> 0.68 us
    dot_general x89 -> x0, matrix products: 157 us -> none  [the longest x74 111 us: product(): jnp.einsum(spec, left_op, right_op, preferred_element_type=jnp.float32)]
    pallas_call x0 -> x5, Pallas kernels: none -> 82.2 us  [the longest x1 26.4 us: on_device(): call(gradient_kernel, 'gradient', shape((D, 2 * D + 128), BF16), pltpu.Pr...]
    all_to_all x0 -> x2, blocking collectives: none -> 75.4 us  [the longest x1 56.7 us: on_device(): part = lax.all_to_all(part, ('z', 'c'), 0, 0).astype(F32).sum(0)]
    add x21 -> x1, other arithmetic: 28 us -> 1.21 us  [on_device(): place = owner * BUFCH + slot]
    convert_element_type x4 -> x0, local copies, waits for them, and re-layouts: 23.9 us -> none  [the longest x1 6.56 us: on_device(): jnp.dot(delivered, w_in, preferred_element_type=jnp.float32)]
    dynamic_update_slice x64 -> x0, local copies, waits for them, and re-layouts: 23.5 us -> none  [the longest x48 22.9 us: on_device(): lax.map(block_grads, (inner_b, write_b, read_b, upstream_b, rates_b, flag...]
    unnamed x72 -> x5, local copies, waits for them, and re-layouts: 20.8 us -> 2.11 us
  transfers between devices with their start and end apart: 6 -> 3, of which waited for: 4 -> 1; matrix products, arithmetic and copies ran while one was open for 15% -> 1% of each run, Pallas kernels for 0% -> 13%
where the time goes in v1:
time: 292 us; the launch traced here: 291 us
  blocking collectives  97.6 us (33%)
  Pallas kernels  82.2 us (28%)
  waiting for transfers between devices  75.2 us (26%)
  between operations  14.1 us (5%)
  starting transfers between devices  11.8 us (4%)
  local copies, waits for them, and re-layouts  6.15 us (2%)
  other arithmetic  4.37 us (1%)
    all_gather x1, waiting for transfers between devices, on_device(): gathered = lax.all_gather(replay[0, 0], ('z', 'c'), axis=0, tiled=True)  74.5 us
    all_to_all x1, blocking collectives, on_device(): part = lax.all_to_all(part, ('z', 'c'), 0, 0).astype(F32).sum(0)  56.7 us
    pallas_call x1, Pallas kernels, on_device(): call(gradient_kernel, 'gradient', shape((D, 2 * D + 128), BF16), pltpu.Pr...  26.4 us
    pallas_call x1, Pallas kernels, on_device(): call(inside_kernel, 'inside', (shape((steps, D), BF16), shape((steps, D),...  23.7 us
    all_gather x1, blocking collectives, on_device(): all_gain = lax.all_gather(gain[:1], TM, axis=0, tiled=True)  22.2 us
    all_to_all x1, blocking collectives, on_device(): part = lax.all_to_all(part.astype(BF16), TM, 0, 0).astype(F32).sum(0)  18.6 us
    pallas_call x1, Pallas kernels, on_device(): call(project_kernel, 'project', (shape((steps, D), BF16), shape((steps, 1...  16.3 us
    pallas_call x1, Pallas kernels, on_device(): call(upstream_kernel, 'upstream', (shape((steps, D), BF16), shape((32, st...  13.8 us
  transfers between devices with their start and end apart: 3, of which 1 were waited for; matrix products, arithmetic and copies ran while one was open for 1% of the time, Pallas kernels for 13%

profile of v1, /device:TPU:0, one launch (start us, length us, event | category | flops | bytes accessed | tf_op | source)
XLA Modules:
  0.0 291.4 jit_solution(10855463435434150783)
XLA Ops:
  7.2 0.0 all-gather.4.cloned.1.call-start
  7.2 0.7 all-gather.4.cloned.1.call-update
  7.9 1.2 bitcast_add_fusion.place
  9.1 13.8 %upstream.1 = (bf16[2048,1024]{1,0:T(8,128)(2,1)}, f32[32,2048]{1,0:T(8,128)}, f32[2048,128]{1,0:T(8,128)}, f32[8,128]{1,0:T(8,128)}) custom-call(s32[8]{0:T(128)} %bitcast.25, f32[16,2048]{1,0:T(8,128)} %bitcast.28, s32[8,1,256]{2,1,0:T(1,128)} %bitcast.29, bf16[1,2048,1024]{2,1,0:T(8,128)(2,1)} %cot.3, bf16[1024,1024]{1,0:T(8,128)(2,1)} %w_out.1), custom_call_target="tpu_custom_call" | custom-call | flops 4294967296 | bytes 12582912 | tf_op jit(solution)/shard_map/upstream/pallas_call | solution.py:252
  22.9 74.5 %all-gather.4.cloned.1.call-done = bf16[1,1,8192,1024]{3,2,1,0:T(8,128)(2,1)} async-done(((bf16[1,1,1024,1024]{3,2,1,0:T(8,128)(2,1)}), bf16[1,1,8192,1024]{3,2,1,0:T(8,128)(2,1)}) %all-gather.4.cloned.1.call-update) | async-done | bytes 16777232 | tf_op jit(solution)/shard_map/all_gather | solution.py:244
  97.4 16.3 %project.1 = (bf16[2048,1024]{1,0:T(8,128)(2,1)}, bf16[2048,128]{1,0:T(8,128)(2,1)}, f32[8,64,1024]{2,1,0:T(8,128)}, f32[8,64,1024]{2,1,0:T(8,128)}, f32[8,16,1024]{2,1,0:T(8,128)}, /*index=5*/bf16[128,1024]{1,0:T(8,128)(2,1)}) custom-call(s32[8]{0:T(128)} %bitcast_add_fusion.place, s32[8]{0:T(128)} %bitcast.26, bf16[32,256,1024]{2,1,0:T(8,128)(2,1)} %bitcast.18, ...), custom_call_target="tpu_custom_call" | custom-call | flops 6442450944 | bytes 20971520 | tf_op jit(solution)/shard_map/project/pallas_call | solution.py:273
  113.7 6.8 %all-to-all-start = ((bf16[16,8,1024]{2,1,0:T(8,128)(2,1)}), bf16[16,8,1024]{2,1,0:T(8,128)(2,1)S(1)}, u32[]{:S(2)}, u32[]{:S(2)}) async-start(bf16[16,8,1024]{2,1,0:T(8,128)(2,1)} %bitcast.23), calls=%async_computation | async-start | bytes 524288 | tf_op jit(solution)/shard_map/all_to_all | solution.py:312
  120.5 0.7 slice_bitcast_fusion
  121.2 22.2 %all-gather.1 = f32[16,1,128]{2,1,0:T(1,128)} all-gather(f32[1,1,128]{2,1,0:T(1,128)S(1)} %slice_bitcast_fusion), channel_id=1, replica_groups=mesh['y'=4,'x'=4,'z'=4,'c'=2] {'y','x'}, dimensions={0}, use_global_device_ids=true | all-gather | bytes 8704 | tf_op jit(solution)/shard_map/all_gather | solution.py:270
  143.5 0.0 all-to-all-done.terms
  143.5 0.0 copy-start.1
  143.5 0.7 copy-done.1
  144.2 2.1 scan.1
  146.3 4.9 %all-to-all-start.1 = ((bf16[16,8,1024]{2,1,0:T(8,128)(2,1)}), bf16[16,8,1024]{2,1,0:T(8,128)(2,1)S(1)}, u32[]{:S(2)}, u32[]{:S(2)}) async-start(bf16[16,8,1024]{2,1,0:T(8,128)(2,1)} %scan.1), calls=%async_computation.1 | async-start | bytes 524288 | tf_op jit(solution)/shard_map/all_to_all | solution.py:327
  151.2 23.7 %inside.1 = (bf16[2048,1024]{1,0:T(8,128)(2,1)}, bf16[2048,1024]{1,0:T(8,128)(2,1)}, bf16[8,256,256]{2,1,0:T(8,128)(2,1)}) custom-call(bf16[2048,1024]{1,0:T(8,128)(2,1)} %get-tuple-element.18.inner, bf16[2048,128]{1,0:T(8,128)(2,1)} %get-tuple-element.19.keys, bf16[2048,1024]{1,0:T(8,128)(2,1)} %get-tuple-element.16.up, f32[32,2048]{1,0:T(8,128)} %get-tuple-element.20.rows, ...), custom_call_target="tpu_custom_call" | custom-call | flops 12884901888 | bytes 18874368 | tf_op jit(solution)/shard_map/inside/pallas_call | solution.py:299
  174.9 0.0 all-to-all-done.1
  174.9 0.0 copy-start
  174.9 0.7 copy-done
  175.6 26.4 %gradient.1 = bf16[1024,2176]{1,0:T(8,128)(2,1)} custom-call(s32[8]{0:T(128)} %bitcast_add_fusion.place, s32[8]{0:T(128)} %bitcast.27, bf16[32,256,1024]{2,1,0:T(8,128)(2,1)} %bitcast.19, bf16[1,2048,1024]{2,1,0:T(8,128)(2,1)} %cot.3, bf16[2048,1024]{1,0:T(8,128)(2,1)} %get-tuple-element.18.inner, bf16[2048,1024]{1,0:T(8,128)(2,1)} %get-tuple-element.16.up, ...), custom_call_target="tpu_custom_call" | custom-call | flops 11274289152 | bytes 41943040 | tf_op jit(solution)/shard_map/gradient/pallas_call | solution.py:332
  202.0 2.8 copy.17
  204.8 56.7 %all_to_all.20 = bf16[8,16,8,2176]{3,2,1,0:T(8,128)(2,1)} all-to-all(bf16[8,16,8,2176]{3,2,1,0:T(8,128)(2,1)S(1)} %bitcast.20), channel_id=1, replica_groups=mesh['y'=4,'x'=4,'z'=4,'c'=2] {'z','c'}, dimensions={0} | all-to-all | bytes 8912896 | tf_op jit(solution)/shard_map/all_to_all | solution.py:373
  261.5 3.1 %reduce_sum.21 = bf16[16,8,2176]{2,1,0:T(8,128)(2,1)S(1)} reduce(bf16[8,16,8,2176]{3,2,1,0:T(8,128)(2,1)} %all_to_all.20, bf16[]{:T(256)} %constant.32.clone.1), dimensions={0}, to_apply=%region_0.1 | reduce | flops 1949696 | bytes 5013506 | tf_op jit(solution)/shard_map/reduce_sum | solution.py:373
  264.6 18.6 %all_to_all.21 = bf16[16,8,2176]{2,1,0:T(8,128)(2,1)S(1)} all-to-all(bf16[16,8,2176]{2,1,0:T(8,128)(2,1)S(1)} %reduce_sum.21), channel_id=1, replica_groups=mesh['y'=4,'x'=4,'z'=4,'c'=2] {'y','x'}, dimensions={0} | all-to-all | bytes 1114112 | tf_op jit(solution)/shard_map/all_to_all | solution.py:374
  283.2 0.1 convert_reduce_fusion
  283.3 0.6 slice.17
  283.9 0.6 fusion
Async XLA Ops:
  7.2 90.2 %all-gather.4.cloned.1.call-start = ((), (), s32[]{:S(2)}) async-start(), calls=%async_computation.4 | async-start | bytes 18874368 | tf_op jit(solution)/shard_map/all_gather | solution.py:244
  113.7 29.8 %all-to-all-start = ((bf16[16,8,1024]{2,1,0:T(8,128)(2,1)}), bf16[16,8,1024]{2,1,0:T(8,128)(2,1)S(1)}, u32[]{:S(2)}, u32[]{:S(2)}) async-start(bf16[16,8,1024]{2,1,0:T(8,128)(2,1)} %bitcast.23), calls=%async_computation | async-start | bytes 524288 | tf_op jit(solution)/shard_map/all_to_all | solution.py:312
  143.5 0.7 copy-start.1
  146.3 28.6 %all-to-all-start.1 = ((bf16[16,8,1024]{2,1,0:T(8,128)(2,1)}), bf16[16,8,1024]{2,1,0:T(8,128)(2,1)S(1)}, u32[]{:S(2)}, u32[]{:S(2)}) async-start(bf16[16,8,1024]{2,1,0:T(8,128)(2,1)} %scan.1), calls=%async_computation.1 | async-start | bytes 524288 | tf_op jit(solution)/shard_map/all_to_all | solution.py:327
  174.9 0.7 copy-start
Sparse Core Ops, SparseCore 0:
  9.7 87.6 all-gather.3
